TPU v7x, 32 devices: a whole 2x2x4 slice. The times are simulated.
32 devices in a mesh: pix: 4 (over z), cell: 8 (over y, x, core).
Axes of the slice: x: 2, y: 2, z: 4, core: 2. Of those that a mesh axis runs over, the one named last changes fastest.
Arguments:
- influence: float32 [32768, 16384], P('pix', 'cell'), as said below
- observed: float32 [32768, 128], P(('pix', 'cell')), may hold values from -6 to 6
Outputs:
- power: float32 [16384, 128], P(('cell', 'pix'))
- residual: float32 [32768, 128], P(('pix', 'cell'))
- gradient: float32 [16384, 128], P(('cell', 'pix'))
Inputs may be any that keep to these rules, and one draw needn't show every extreme that they name: A dense influence matrix with independent entries.
All inputs are finite; a program needn't handle non-finite values.
Results may differ from a plain program's by a relative error of at most 0.0003.
Values sent between devices are 32-bit elements; how exact they have to be, the bound alone decides.
No kernel may reach another device: no remote copies, remote signals or barrier semaphores. Data moves between devices by JAX's collectives and lax.ppermute only.
A program may use at most 128 MiB of HBM per device.

v0:
```python
import jax
import jax.numpy as jnp
from jax import lax
from jax.sharding import PartitionSpec as P

ITERS = 2


def body(influence, observed):
    high = lax.Precision.HIGHEST

    def adjoint(residual):
        whole = lax.all_gather(residual, "cell", axis=0, tiled=True)
        return lax.psum_scatter(
            lax.dot_general(
                influence,
                whole,
                (((0,), (0,)), ((), ())),
                precision=high,
                preferred_element_type=jnp.float32,
            ),
            "pix",
            scatter_dimension=0,
            tiled=True,
        )

    def gradient_squares(gradient):
        local_sum = jnp.sum(gradient * gradient, axis=0)
        return lax.psum(local_sum, ("pix", "cell"))

    residual = observed
    gradient = adjoint(residual)
    gamma = gradient_squares(gradient)
    direction = gradient
    power = jnp.zeros_like(gradient)
    for step in range(ITERS):
        forward_whole = lax.all_gather(direction, "pix", axis=0, tiled=True)
        image = lax.psum_scatter(
            jnp.dot(influence, forward_whole, precision=high, preferred_element_type=jnp.float32),
            "cell",
            scatter_dimension=0,
            tiled=True,
        )
        image_local_sum = jnp.sum(image * image, axis=0)
        alpha = gamma / lax.psum(image_local_sum, ("pix", "cell"))
        power = power + alpha * direction
        residual = residual - alpha * image
        gradient = adjoint(residual)
        fresh = gradient_squares(gradient)
        direction = gradient + fresh / gamma * direction
        gamma = fresh
    return (power, residual, gradient)


def solution(mesh):
    in_specs = (P("pix", "cell"), P(("pix", "cell"), None))
    out_specs = (P(("cell", "pix"), None), P(("pix", "cell"), None), P(("cell", "pix"), None))
    return jax.shard_map(body, mesh=mesh, in_specs=in_specs, out_specs=out_specs, check_vma=False)
```

profile of v0, /device:TPU:0, one launch (start us, length us, event | category | flops | bytes accessed | tf_op | source)
XLA Modules:
  0.0 935.7 jit_solution(17899036911111349830)
XLA Ops:
  7.2 0.7 all-gather.6.cloned.1.call-update
  8.0 41.4 %all-gather.6.cloned.1.call-done = f32[8192,128]{1,0:T(8,128)} async-done(((f32[1024,128]{1,0:T(8,128)}), f32[8192,128]{1,0:T(8,128)}) %all-gather.6.cloned.1.call-update) | async-done | bytes 4194320 | tf_op jit(solution)/shard_map/all_gather | solution.py:13
  49.3 109.9 %fusion = f32[2048,128]{1,0:T(8,128)} fusion(f32[8192,2048]{1,0:T(8,128)} %param.2, f32[8192,128]{1,0:T(8,128)} %all-gather.6.cloned.1.call-done), kind=kOutput, calls=%fused_computation.12 | convolution fusion | flops 25769803776 | bytes 72351744 | tf_op jit(solution)/shard_map/dot_general | solution.py:15
  159.4 27.2 %reduce-scatter.6.cloned.1.call-done = f32[512,128]{1,0:T(8,128)} async-done(((f32[2048,128]{1,0:T(8,128)}), f32[512,128]{1,0:T(8,128)}) %reduce-scatter.6.cloned.1.call-update) | async-done | bytes 262160 | tf_op jit(solution)/shard_map/reduce_scatter | solution.py:14
  186.7 28.2 %all-gather.8.cloned.1.call-done = f32[2048,128]{1,0:T(8,128)} async-done(((f32[512,128]{1,0:T(8,128)}), f32[2048,128]{1,0:T(8,128)}) %all-gather.8.cloned.1.call-update) | async-done | bytes 1048592 | tf_op jit(solution)/shard_map/all_gather | solution.py:37
  214.9 87.7 %convolution_bitcast_fusion.1 = f32[8192,128]{0,1:T(8,128)} fusion(f32[2048,128]{1,0:T(8,128)} %all-gather.8.cloned.1.call-done, f32[8192,2048]{1,0:T(8,128)} %param.2), kind=kOutput, calls=%fused_computation.1 | convolution fusion | flops 25769803776 | bytes 72351744 | tf_op jit(solution)/shard_map/dot_general | solution.py:39
  302.6 0.0 all-gather.10.cloned.1.call-start
  302.6 0.2 copy.5
  302.8 0.1 multiply_reduce_fusion.3
  302.9 50.6 %reduce-scatter.8.cloned.1.call-done = f32[1024,128]{0,1:T(8,128)} async-done(((f32[8192,128]{0,1:T(8,128)}), f32[1024,128]{0,1:T(8,128)}) %reduce-scatter.8.cloned.1.call-update) | async-done | bytes 524304 | tf_op jit(solution)/shard_map/reduce_scatter | solution.py:38
  353.5 1.2 multiply_reduce_fusion.1
  354.7 39.3 %all-reduce = (f32[128]{0:T(128)S(1)}, f32[128]{0:T(128)S(1)}) all-reduce(f32[128]{0:T(128)S(1)} %multiply_reduce_fusion.3, f32[128]{0:T(128)S(1)} %multiply_reduce_fusion.1), channel_id=1, replica_groups=mesh['pix'=4,'cell'=8] {'pix','cell'}, use_global_device_ids=true, to_apply=%region_2.0 | all-reduce | flops 256 | bytes 2048 | tf_op jit(solution)/shard_map/psum | solution.py:29
  394.1 2.0 multiply_subtract_fusion.1
  396.1 37.5 %all-gather.10.cloned.1.call-done = f32[8192,128]{0,1:T(8,128)} async-done(((f32[1024,128]{0,1:T(8,128)}), f32[8192,128]{0,1:T(8,128)}) %all-gather.10.cloned.1.call-update) | async-done | bytes 4194320 | tf_op jit(solution)/shard_map/all_gather | solution.py:13
  433.6 110.1 %convolution_bitcast_fusion.3 = f32[2048,128]{1,0:T(8,128)} fusion(f32[8192,128]{0,1:T(8,128)} %all-gather.10.cloned.1.call-done, f32[8192,2048]{1,0:T(8,128)} %param.2), kind=kOutput, calls=%fused_computation.3 | convolution fusion | flops 25769803776 | bytes 72351744 | tf_op jit(solution)/shard_map/dot_general | solution.py:15
  543.7 0.0 all-gather.12.cloned.1.call-start
  543.8 27.2 %reduce-scatter.10.cloned.1.call-done = f32[512,128]{1,0:T(8,128)} async-done(((f32[2048,128]{1,0:T(8,128)}), f32[512,128]{1,0:T(8,128)}) %reduce-scatter.10.cloned.1.call-update) | async-done | bytes 262160 | tf_op jit(solution)/shard_map/reduce_scatter | solution.py:14
  571.0 1.0 multiply_reduce_fusion.2
  572.1 38.9 %psum.30 = f32[128]{0:T(128)S(1)} all-reduce(f32[128]{0:T(128)S(1)} %multiply_reduce_fusion.2), channel_id=1, replica_groups=mesh['pix'=4,'cell'=8] {'pix','cell'}, use_global_device_ids=true, to_apply=%region_8.0 | all-reduce | flops 128 | bytes 1024 | tf_op jit(solution)/shard_map/psum | solution.py:29
  610.9 1.7 multiply_add_fusion.1
  612.7 27.8 %all-gather.12.cloned.1.call-done = f32[2048,128]{1,0:T(8,128)} async-done(((f32[512,128]{1,0:T(8,128)}), f32[2048,128]{1,0:T(8,128)}) %all-gather.12.cloned.1.call-update) | async-done | bytes 1048592 | tf_op jit(solution)/shard_map/all_gather | solution.py:37
  640.5 77.3 %convolution_bitcast_fusion = f32[8192,128]{0,1:T(8,128)} fusion(f32[2048,128]{1,0:T(8,128)} %all-gather.12.cloned.1.call-done, f32[8192,2048]{1,0:T(8,128)} %param.2), kind=kOutput, calls=%fused_computation | convolution fusion | flops 25769803776 | bytes 72351744 | tf_op jit(solution)/shard_map/dot_general | solution.py:39
  717.8 50.9 %reduce-scatter.12.cloned.1.call-done = f32[1024,128]{0,1:T(8,128)} async-done(((f32[8192,128]{0,1:T(8,128)}), f32[1024,128]{0,1:T(8,128)}) %reduce-scatter.12.cloned.1.call-update) | async-done | bytes 524304 | tf_op jit(solution)/shard_map/reduce_scatter | solution.py:38
  768.8 1.2 multiply_reduce_fusion
  769.9 39.3 %psum.31 = f32[128]{0:T(128)S(1)} all-reduce(f32[128]{0:T(128)S(1)} %multiply_reduce_fusion), channel_id=1, replica_groups=mesh['pix'=4,'cell'=8] {'pix','cell'}, use_global_device_ids=true, to_apply=%region_11.0 | all-reduce | flops 128 | bytes 1024 | tf_op jit(solution)/shard_map/psum | solution.py:45
  809.3 2.0 multiply_subtract_fusion
  811.3 37.5 %all-gather.14.cloned.1.call-done = f32[8192,128]{0,1:T(8,128)} async-done(((f32[1024,128]{0,1:T(8,128)}), f32[8192,128]{0,1:T(8,128)}) %all-gather.14.cloned.1.call-update) | async-done | bytes 4194320 | tf_op jit(solution)/shard_map/all_gather | solution.py:13
  848.9 50.5 %convolution_bitcast_fusion.2 = f32[2048,128]{0,1:T(8,128)} fusion(f32[8192,128]{0,1:T(8,128)} %all-gather.14.cloned.1.call-done, f32[8192,2048]{1,0:T(8,128)} %param.2), kind=kOutput, calls=%fused_computation.2 | convolution fusion | flops 25769803776 | bytes 72351744 | tf_op jit(solution)/shard_map/dot_general | solution.py:15
  899.4 1.0 copy.7
  900.4 0.7 multiply_add_fusion
  901.1 25.6 %reduce-scatter.14.cloned.1.call-done = f32[512,128]{0,1:T(8,128)} async-done(((f32[2048,128]{0,1:T(8,128)}), f32[512,128]{0,1:T(8,128)}) %reduce-scatter.14.cloned.1.call-update) | async-done | bytes 262160 | tf_op jit(solution)/shard_map/reduce_scatter | solution.py:14
  926.7 1.8 copy.8
  (30 shorter events, 0.5 us)
Async XLA Ops:
  7.2 42.2 %all-gather.6.cloned.1.call-start = ((), (), s32[]{:S(2)}) async-start(), calls=%async_computation.5 | async-start | bytes 4718592 | tf_op jit(solution)/shard_map/all_gather | solution.py:13
  7.9 294.7 %copy-start.4 = (f32[1024,128]{1,0:T(8,128)S(1)}, f32[1024,128]{1,0:T(8,128)}, u32[]{:S(2)}) copy-start(f32[1024,128]{1,0:T(8,128)} %param.3) | copy-start | bytes 1572868
  7.9 178.7 %reduce-scatter.6.cloned.1.call-start = ((), (), s32[]{:S(2)}) async-start(), calls=%async_computation.6 | async-start | bytes 1310720 | tf_op jit(solution)/shard_map/reduce_scatter | solution.py:14
  159.3 55.6 %all-gather.8.cloned.1.call-start = ((), (), s32[]{:S(2)}) async-start(), calls=%async_computation.7 | async-start | bytes 1310720 | tf_op jit(solution)/shard_map/all_gather | solution.py:37
  186.6 116.2 %copy-start.2 = (f32[512,128]{1,0:T(8,128)S(1)}, f32[512,128]{1,0:T(8,128)}, u32[]{:S(2)}) copy-start(f32[512,128]{1,0:T(8,128)} %reduce-scatter.6.cloned.1.call-done) | copy-start | bytes 786436
  186.6 166.9 %reduce-scatter.8.cloned.1.call-start = ((), (), s32[]{:S(2)}) async-start(), calls=%async_computation.8 | async-start | bytes 4718592 | tf_op jit(solution)/shard_map/reduce_scatter | solution.py:38
  302.6 131.1 %all-gather.10.cloned.1.call-start = ((), (), s32[]{:S(2)}) async-start(), calls=%async_computation.9 | async-start | bytes 4718592 | tf_op jit(solution)/shard_map/all_gather | solution.py:13
  396.0 413.2 %copy-start = (f32[1024,128]{0,1:T(8,128)S(1)}, f32[1024,128]{0,1:T(8,128)}, u32[]{:S(2)}) copy-start(f32[1024,128]{0,1:T(8,128)} %multiply_subtract_fusion.1) | copy-start | bytes 1572868
  396.1 175.0 %reduce-scatter.10.cloned.1.call-start = ((), (), s32[]{:S(2)}) async-start(), calls=%async_computation.10 | async-start | bytes 1310720 | tf_op jit(solution)/shard_map/reduce_scatter | solution.py:14
  543.7 96.7 %all-gather.12.cloned.1.call-start = ((), (), s32[]{:S(2)}) async-start(), calls=%async_computation.11 | async-start | bytes 1310720 | tf_op jit(solution)/shard_map/all_gather | solution.py:37
  612.6 156.1 %reduce-scatter.12.cloned.1.call-start = ((), (), s32[]{:S(2)}) async-start(), calls=%async_computation.12 | async-start | bytes 4718592 | tf_op jit(solution)/shard_map/reduce_scatter | solution.py:38
  717.8 182.6 %copy-start.3 = (f32[512,128]{1,0:T(8,128)S(1)}, f32[512,128]{1,0:T(8,128)}, u32[]{:S(2)}) copy-start(f32[512,128]{1,0:T(8,128)} %multiply_add_fusion.1) | copy-start | bytes 786436
  717.8 131.1 %all-gather.14.cloned.1.call-start = ((), (), s32[]{:S(2)}) async-start(), calls=%async_computation.13 | async-start | bytes 4718592 | tf_op jit(solution)/shard_map/all_gather | solution.py:13
  811.2 88.1 %copy-start.1 = (f32[1024,128]{0,1:T(8,128)S(1)}, f32[1024,128]{0,1:T(8,128)}, u32[]{:S(2)}) copy-start(f32[1024,128]{0,1:T(8,128)} %multiply_subtract_fusion) | copy-start | bytes 1572868
  811.3 115.4 %reduce-scatter.14.cloned.1.call-start = ((), (), s32[]{:S(2)}) async-start(), calls=%async_computation.14 | async-start | bytes 1310720 | tf_op jit(solution)/shard_map/reduce_scatter | solution.py:14
Sparse Core Ops, SparseCore 0:
  9.9 39.4 all-gather.5
  159.4 27.1 reduce-scatter.5
  188.3 26.5 all-gather.7
  302.7 50.8 reduce-scatter.7
  396.2 37.4 all-gather.9
  543.9 27.1 reduce-scatter.9
  612.8 27.6 all-gather.11
  717.9 50.8 reduce-scatter.11
  811.4 37.4 all-gather.13
  899.5 27.1 reduce-scatter.13
where the time goes:
time: 946 us; the launch traced here: 936 us
  matrix products  435 us (46%)
  waiting for transfers between devices  355 us (38%)
  blocking collectives  118 us (12%)
  between operations  14.7 us (2%)
  other arithmetic  9.77 us (1%)
    dot_general x3, matrix products, adjoint(): lax.dot_general(influence, whole, (((0,), (0,)), ((), ())), precision=hig...  271 us
    dot_general x2, matrix products, body(): jnp.dot(influence, forward_whole, precision=high, preferred_element_type=...  165 us
    all_gather x3, waiting for transfers between devices, adjoint(): whole = lax.all_gather(residual, 'cell', axis=0, tiled=True)  116 us
    reduce_scatter x2, waiting for transfers between devices, body(): lax.psum_scatter(jnp.dot(influence, forward_whole, precision=high, prefer...  102 us
    reduce_scatter x3, waiting for transfers between devices, adjoint(): lax.psum_scatter(lax.dot_general(influence, whole, (((0,), (0,)), ((), ()...  80.1 us
    psum x2, blocking collectives, gradient_squares(): return lax.psum(local_sum, ('pix', 'cell'))  78.2 us
    all_gather x2, waiting for transfers between devices, body(): forward_whole = lax.all_gather(direction, 'pix', axis=0, tiled=True)  56 us
    psum x1, blocking collectives, body(): alpha = gamma / lax.psum(image_local_sum, ('pix', 'cell'))  39.3 us
  transfers between devices with their start and end apart: 10, of which 10 were waited for; matrix products, arithmetic and copies ran while one was open for 0% of the time, Pallas kernels for 0%

commit v1 on v0

v1 whole, which is shorter than its diff:
```python
import functools

import jax
import jax.numpy as jnp
from jax import lax
from jax.experimental import pallas as pl
from jax.experimental.pallas import tpu as pltpu
from jax.sharding import PartitionSpec as P

ITERS = 2
BLOCK_ROWS = 512
VMEM_LIMIT = 50 * 2**20
f32 = jnp.float32
bf16 = jnp.bfloat16


def split(x):
    high = x.astype(bf16)
    return high, (x - high.astype(f32)).astype(bf16)


def block_rows(chunk_rows):
    return min(BLOCK_ROWS, chunk_rows)


def cost(products, rows, cols, frames):
    return pl.CostEstimate(
        flops=2 * 3 * products * rows * cols * frames,
        bytes_accessed=4 * products * rows * cols,
        transcendentals=0,
    )


def forward_kernel(parts, per_chunk, index_ref, *refs):
    x_refs, a_ref, out_ref, cat_ref, sum_ref = refs[:parts], refs[parts], refs[parts + 1], refs[parts + 2], refs[parts + 3]
    step = pl.program_id(0)
    frames = x_refs[0].shape[1]
    cells = x_refs[0].shape[0]

    @pl.when(step == 0)
    def _():
        total = jnp.zeros((1, frames), f32)
        for part in range(parts):
            x = x_refs[part][...]
            high, low = split(x)
            start = pl.multiple_of((index_ref[0] ^ part) * cells, cells)
            cat_ref[pl.ds(start, cells), :frames] = high
            cat_ref[pl.ds(start, cells), frames:] = low
            total = total + jnp.sum(x * x, axis=0, keepdims=True)
        sum_ref[...] = jnp.broadcast_to(total, sum_ref.shape)

    high, low = split(a_ref[...])
    both = jnp.dot(high, cat_ref[...], preferred_element_type=f32)
    rows = a_ref.shape[0]
    value = both[:, :frames] + both[:, frames:] + jnp.dot(low, cat_ref[:, :frames], preferred_element_type=f32)
    if per_chunk == 1:
        out_ref[0, :rows, :] = value
    else:
        start = pl.multiple_of(lax.rem(step, per_chunk) * rows, rows)
        out_ref[0, pl.ds(start, rows), :] = value
    out_ref[0, rows * per_chunk :, :] = sum_ref[...]


def forward_call(influence, x_parts, me_pix, chunks, chunk_rows):
    count = chunks.shape[0]
    cols = influence.shape[1]
    frames = x_parts[0].shape[1]
    rows = block_rows(chunk_rows)
    per_chunk = chunk_rows // rows
    index = jnp.concatenate([me_pix[None], chunks]).astype(jnp.int32)
    whole = pl.BlockSpec(memory_space=pltpu.VMEM)
    return pl.pallas_call(
        functools.partial(forward_kernel, len(x_parts), per_chunk),
        grid_spec=pltpu.PrefetchScalarGridSpec(
            num_scalar_prefetch=1,
            grid=(count * per_chunk,),
            in_specs=[whole] * len(x_parts)
            + [pl.BlockSpec((rows, cols), lambda s, ix: (ix[1 + s // per_chunk] * per_chunk + s % per_chunk, 0))],
            out_specs=pl.BlockSpec((1, chunk_rows + 8, frames), lambda s, ix: (s // per_chunk, 0, 0)),
            scratch_shapes=[pltpu.VMEM((cols, 2 * frames), bf16), pltpu.VMEM((8, frames), f32)],
        ),
        out_shape=jax.ShapeDtypeStruct((count, chunk_rows + 8, frames), f32),
        compiler_params=pltpu.CompilerParams(vmem_limit_bytes=VMEM_LIMIT),
        cost_estimate=cost(count, chunk_rows, cols, frames),
        name="forward_product",
    )(index, *x_parts, influence)


def adjoint_kernel(count, per_chunk, first, last, parts, index_ref, *refs):
    r_refs = refs[:count]
    a_ref = refs[count]
    refs = refs[count + 1 :]
    if not first:
        acc_in, sum_in = refs[0], refs[1]
        refs = refs[2:]
    if last:
        out_ref, acc, sums, cat_ref, flat = refs
    else:
        acc, sums, cat_ref = refs
    step = pl.program_id(0)
    frames = r_refs[0].shape[1]
    rows = a_ref.shape[0]

    @pl.when(step == 0)
    def _():
        total = jnp.zeros((1, frames), f32)
        for i in range(count):
            r = r_refs[i][...]
            total = total + jnp.sum(r * r, axis=0, keepdims=True)
            for k in range(per_chunk):
                high, low = split(r[k * rows : (k + 1) * rows].T)
                cat_ref[i * per_chunk + k, :frames, :] = high
                cat_ref[i * per_chunk + k, frames:, :] = low
        if first:
            sums[...] = jnp.broadcast_to(total, sums.shape)
            acc[...] = jnp.zeros_like(acc)
        else:
            sums[...] = sum_in[...] + total
            acc[...] = acc_in[...]

    high, low = split(a_ref[...])
    both = jnp.dot(cat_ref[step], high, preferred_element_type=f32)
    other = jnp.dot(cat_ref[step, :frames, :], low, preferred_element_type=f32)
    acc[...] += both[:frames] + both[frames:] + other

    if last:

        @pl.when(step == count * per_chunk - 1)
        def _():
            cells = out_ref.shape[1] - 8
            flat[...] = acc[...].T
            for part in range(parts):
                start = pl.multiple_of((index_ref[0] ^ part) * cells, cells)
                out_ref[part, :cells, :] = flat[pl.ds(start, cells), :]
                out_ref[part, cells:, :] = sums[...]


def adjoint_call(influence, r_parts, me_pix, chunks, carry, last, parts):
    count = len(r_parts)
    cols = influence.shape[1]
    chunk_rows, frames = r_parts[0].shape
    rows = block_rows(chunk_rows)
    per_chunk = chunk_rows // rows
    index = jnp.concatenate([me_pix[None], chunks]).astype(jnp.int32)
    whole = pl.BlockSpec(memory_space=pltpu.VMEM)
    cat = pltpu.VMEM((count * per_chunk, 2 * frames, rows), bf16)
    carried = (jax.ShapeDtypeStruct((frames, cols), f32), jax.ShapeDtypeStruct((8, frames), f32))
    if last:
        out_shape = jax.ShapeDtypeStruct((parts, cols // parts + 8, frames), f32)
        out_specs = whole
        scratch = [pltpu.VMEM(c.shape, f32) for c in carried] + [cat, pltpu.VMEM((cols, frames), f32)]
    else:
        out_shape = carried
        out_specs = (whole, whole)
        scratch = [cat]
    return pl.pallas_call(
        functools.partial(adjoint_kernel, count, per_chunk, carry is None, last, parts),
        grid_spec=pltpu.PrefetchScalarGridSpec(
            num_scalar_prefetch=1,
            grid=(count * per_chunk,),
            in_specs=[whole] * count
            + [pl.BlockSpec((rows, cols), lambda s, ix: (ix[1 + s // per_chunk] * per_chunk + s % per_chunk, 0))]
            + [whole] * (0 if carry is None else 2),
            out_specs=out_specs,
            scratch_shapes=scratch,
        ),
        out_shape=out_shape,
        compiler_params=pltpu.CompilerParams(vmem_limit_bytes=VMEM_LIMIT),
        cost_estimate=cost(count, chunk_rows, cols, frames),
        name="adjoint_product",
    )(index, *r_parts, influence, *(() if carry is None else carry))


def solution(mesh):
    cell_size, pix_size = mesh.shape["cell"], mesh.shape["pix"]
    bits = cell_size.bit_length() - 1
    stages = bits - 1
    group = cell_size // 2
    order = (list(range(1, bits)), list(range(bits - 1, 0, -1)))

    def offset(core, w):
        return sum(1 << order[core][j] for j in range(stages) if (w >> (stages - 1 - j)) & 1)

    offsets = [[offset(core, w) for w in range(group)] for core in range(2)]
    stage_perm = [[(i, i ^ (1 << order[i & 1][j])) for i in range(cell_size)] for j in range(stages)]
    core_perm = [(i, i ^ 1) for i in range(cell_size)]

    def body(influence, observed):
        chunk_rows = influence.shape[0] // cell_size
        me_cell, me_pix = lax.axis_index("cell"), lax.axis_index("pix")
        even = (me_cell & 1) == 0
        table = jnp.array(offsets, jnp.int32)
        own = me_cell ^ jnp.where(even, table[0], table[1])
        other = (me_cell ^ 1) ^ jnp.where(even, table[1], table[0])

        def adjoint(residual):
            mine = [residual]
            waves = []
            for j in reversed(range(stages)):
                mine = mine + [lax.ppermute(piece, "cell", stage_perm[j]) for piece in mine]
            theirs = [lax.ppermute(piece, "cell", core_perm) for piece in mine]
            cuts = [0, 1, max(1, group - 1), group]
            carry = None
            for lo, hi in zip(cuts[:-1], cuts[1:]):
                if lo == hi:
                    continue
                last = hi == group
                carry = adjoint_call(
                    influence,
                    mine[lo:hi] + theirs[lo:hi],
                    me_pix,
                    jnp.concatenate([own[lo:hi], other[lo:hi]]),
                    carry,
                    last,
                    pix_size,
                )
            total = carry[0]
            for part in range(1, pix_size):
                total = total + lax.ppermute(carry[part], "pix", [(i, i ^ part) for i in range(pix_size)])
            return total[:-8], total[-8]

        def forward(gradient):
            parts = [gradient] + [
                lax.ppermute(gradient, "pix", [(i, i ^ part) for i in range(pix_size)]) for part in range(1, pix_size)
            ]
            call = functools.partial(forward_call, influence, parts, me_pix)
            sent = lax.ppermute(call(other, chunk_rows), "cell", core_perm)
            half = group // 2
            away, home = call(own[half:], chunk_rows), call(own[:half], chunk_rows)
            away, home = away + sent[half:], home + sent[:half]
            for j in range(stages):
                home = home + lax.ppermute(away, "cell", stage_perm[j])
                half = home.shape[0] // 2
                away, home = home[half:], home[: max(half, 1)]
            return home[0, :-8], home[0, -8]

        gradient, _ = adjoint(observed)
        image, gamma = forward(gradient)
        direction = gradient
        residual = observed
        power = jnp.zeros_like(gradient)
        for step in range(ITERS):
            back, squares = adjoint(image)
            alpha = gamma / squares
            power = power + alpha * direction
            residual = residual - alpha * image
            gradient = gradient - alpha * back
            if step + 1 < ITERS:
                fresh_image, fresh = forward(gradient)
                beta = fresh / gamma
                image = fresh_image + beta * image
                direction = gradient + beta * direction
                gamma = fresh
        return (power, residual, gradient)

    in_specs = (P("pix", "cell"), P(("pix", "cell"), None))
    out_specs = (P(("cell", "pix"), None), P(("pix", "cell"), None), P(("cell", "pix"), None))
    return jax.shard_map(body, mesh=mesh, in_specs=in_specs, out_specs=out_specs, check_vma=False)
```

time: 946 us -> 400 us (0.42)
  matrix products: 435 us -> 0 us
  waiting for transfers between devices: 355 us -> 149 us
  Pallas kernels: 0 us -> 178 us
  blocking collectives: 118 us -> 0 us
  starting transfers between devices: 0.41 us -> 55.8 us
  between operations: 14.7 us -> 0.99 us
    dot_general x5 -> x0, matrix products: 435 us -> none  [the longest x3 271 us: adjoint(): lax.dot_general(influence, whole, (((0,), (0,)), ((), ())), precision=hig...]
    reduce_scatter x5 -> x0, waiting for transfers between devices: 182 us -> none  [the longest x2 102 us: body(): lax.psum_scatter(jnp.dot(influence, forward_whole, precision=high, prefer...]
    pallas_call x0 -> x15, Pallas kernels: none -> 178 us  [the longest x9 107 us: adjoint_call(): pl.pallas_call(functools.partial(adjoint_kernel, count, per_chunk, carry...]
    all_gather x5 -> x0, waiting for transfers between devices: 172 us -> none  [the longest x3 116 us: adjoint(): whole = lax.all_gather(residual, 'cell', axis=0, tiled=True)]
    ppermute x0 -> x42, waiting for transfers between devices: none -> 149 us  [the longest x9 57.2 us: adjoint(): lax.ppermute(carry[part], 'pix', [(i, i ^ part) for i in range(pix_size)])]
    psum x3 -> x0, blocking collectives: 118 us -> none  [the longest x2 78.2 us: gradient_squares(): return lax.psum(local_sum, ('pix', 'cell'))]
    ppermute x0 -> x42, starting transfers between devices: none -> 55.8 us  [the longest x9 17.8 us: adjoint(): lax.ppermute(carry[part], 'pix', [(i, i ^ part) for i in range(pix_size)])]
  transfers between devices with their start and end apart: 10 -> 42, of which waited for: 10 -> 17; matrix products, arithmetic and copies ran while one was open for 0% -> 1% of each run, Pallas kernels for 0% -> 29%
where the time goes in v1:
time: 400 us; the launch traced here: 396 us
  Pallas kernels  178 us (44%)
  waiting for transfers between devices  149 us (37%)
  starting transfers between devices  55.8 us (14%)
  other arithmetic  6.79 us (2%)
  local copies, waits for them, and re-layouts  5.11 us (1%)
    pallas_call x9, Pallas kernels, adjoint_call(): pl.pallas_call(functools.partial(adjoint_kernel, count, per_chunk, carry...  107 us
    pallas_call x6, Pallas kernels, forward_call(): pl.pallas_call(functools.partial(forward_kernel, len(x_parts), per_chunk)...  70.8 us
    ppermute x9, waiting for transfers between devices, adjoint(): lax.ppermute(carry[part], 'pix', [(i, i ^ part) for i in range(pix_size)])  57.2 us
    ppermute x6, waiting for transfers between devices, forward(): lax.ppermute(gradient, 'pix', [(i, i ^ part) for i in range(pix_size)])  37.7 us
    ppermute x9, waiting for transfers between devices, adjoint(): mine = mine + [lax.ppermute(piece, 'cell', stage_perm[j]) for piece in mine]  31.7 us
    ppermute x4, waiting for transfers between devices, forward(): home = home + lax.ppermute(away, 'cell', stage_perm[j])  22.5 us
    ppermute x9, starting transfers between devices, adjoint(): lax.ppermute(carry[part], 'pix', [(i, i ^ part) for i in range(pix_size)])  17.8 us
    ppermute x6, starting transfers between devices, forward(): lax.ppermute(gradient, 'pix', [(i, i ^ part) for i in range(pix_size)])  15.6 us
  transfers between devices with their start and end apart: 42, of which 17 were waited for; matrix products, arithmetic and copies ran while one was open for 1% of the time, Pallas kernels for 29%

profile of v1, /device:TPU:0, one launch (start us, length us, event | category | flops | bytes accessed | tf_op | source)
XLA Modules:
  0.0 396.2 jit_solution(1418661944936393137)
XLA Ops:
  8.0 7.7 %collective-permute-done.refs_0_ = f32[1024,128]{1,0:T(8,128)S(1)} collective-permute-done((f32[1024,128]{1,0:T(8,128)}, f32[1024,128]{1,0:T(8,128)S(1)}, u32[]{:S(2)}, u32[]{:S(2)}) %collective-permute-start) | collective-permute-done | bytes 524320 | tf_op jit(solution)/shard_map/ppermute | solution.py:200
  20.9 9.2 %adjoint_product.9 = (f32[128,2048]{1,0:T(8,128)S(1)}, f32[8,128]{1,0:T(8,128)S(1)}) custom-call(s32[3]{0:T(128)S(1)} %pad_add_fusion.3.index_ref, f32[1024,128]{1,0:T(8,128)S(1)} %copy-done, f32[1024,128]{1,0:T(8,128)S(1)} %collective-permute-done.6.refs_1_, f32[8192,2048]{1,0:T(8,128)} %refs_2_.11), custom_call_target="tpu_custom_call" | custom-call | flops 3221225472 | bytes 16777216 | tf_op jit(solution)/shard_map/adjoint_product/pallas_call | solution.py:156
  31.5 16.8 %adjoint_product.10 = (f32[128,2048]{1,0:T(8,128)S(1)}, f32[8,128]{1,0:T(8,128)S(1)}) custom-call(s32[5]{0:T(128)S(1)} %pad_add_fusion.2.index_ref, f32[1024,128]{1,0:T(8,128)S(1)} %collective-permute-done.refs_0_, f32[1024,128]{1,0:T(8,128)S(1)} %collective-permute-done.3.refs_1_, f32[1024,128]{1,0:T(8,128)S(1)} %collective-permute-done.4.refs_2_, ...), custom_call_target="tpu_custom_call" | custom-call | flops 6442450944 | bytes 33554432 | tf_op jit(solution)/shard_map/adjoint_product/pallas_call | solution.py:156
  48.3 9.7 %adjoint_product.11 = f32[4,520,128]{2,1,0:T(8,128)S(1)} custom-call(s32[3]{0:T(128)S(1)} %pad_add_fusion.1.index_ref, f32[1024,128]{1,0:T(8,128)S(1)} %collective-permute-done.1.refs_0_, f32[1024,128]{1,0:T(8,128)S(1)} %collective-permute-done.2.refs_1_, f32[8192,2048]{1,0:T(8,128)} %refs_2_.11, f32[128,2048]{1,0:T(8,128)S(1)} %get-tuple-element.17.refs_3_, ...), custom_call_target="tpu_custom_call" | custom-call | flops 3221225472 | bytes 16777216 | tf_op jit(solution)/shard_map/adjoint_product/pallas_call | solution.py:156
  62.6 9.1 %collective-permute-done.7 = f32[520,128]{1,0:T(8,128)S(1)} collective-permute-done((f32[520,128]{1,0:T(8,128)S(1)}, f32[520,128]{1,0:T(8,128)S(1)}, u32[]{:S(2)}, u32[]{:S(2)}) %collective-permute-start.7) | collective-permute-done | bytes 266272 | tf_op jit(solution)/shard_map/ppermute | solution.py:219
  71.6 9.9 %collective-permute-done.8 = f32[520,128]{1,0:T(8,128)S(1)} collective-permute-done((f32[520,128]{1,0:T(8,128)S(1)}, f32[520,128]{1,0:T(8,128)S(1)}, u32[]{:S(2)}, u32[]{:S(2)}) %collective-permute-start.8) | collective-permute-done | bytes 266272 | tf_op jit(solution)/shard_map/ppermute | solution.py:219
  81.7 5.1 %collective-permute-start.10 = (f32[512,128]{1,0:T(8,128)S(1)}, f32[512,128]{1,0:T(8,128)S(1)}, u32[]{:S(2)}, u32[]{:S(2)}) collective-permute-start(f32[512,128]{1,0:T(8,128)S(1)} %slice_add_fusion.6.refs_0_), channel_id=1, source_target_pairs={{0,8},{8,0},{16,24},{24,16},{1,9},{9,1},{17,25},{25,17},{2,10},{10... | collective-permute-start | bytes 786440 | tf_op jit(solution)/shard_map/ppermute | solution.py:224
  89.3 7.1 %collective-permute-done.10.refs_1_ = f32[512,128]{1,0:T(8,128)S(1)} collective-permute-done((f32[512,128]{1,0:T(8,128)S(1)}, f32[512,128]{1,0:T(8,128)S(1)}, u32[]{:S(2)}, u32[]{:S(2)}) %collective-permute-start.10) | collective-permute-done | bytes 262176 | tf_op jit(solution)/shard_map/ppermute | solution.py:224
  96.4 11.7 %collective-permute-done.11.refs_2_ = f32[512,128]{1,0:T(8,128)S(1)} collective-permute-done((f32[512,128]{1,0:T(8,128)S(1)}, f32[512,128]{1,0:T(8,128)S(1)}, u32[]{:S(2)}, u32[]{:S(2)}) %collective-permute-start.11) | collective-permute-done | bytes 262176 | tf_op jit(solution)/shard_map/ppermute | solution.py:224
  108.1 16.7 %forward_product.7 = f32[4,1032,128]{2,1,0:T(8,128)S(1)} custom-call(s32[5]{0:T(128)S(1)} %pad_add_fusion.4.index_ref, f32[512,128]{1,0:T(8,128)S(1)} %slice_add_fusion.6.refs_0_, f32[512,128]{1,0:T(8,128)S(1)} %collective-permute-done.10.refs_1_, f32[512,128]{1,0:T(8,128)S(1)} %collective-permute-done.11.refs_2_, ...), custom_call_target="tpu_custom_call" | custom-call | flops 6442450944 | bytes 33554432 | tf_op jit(solution)/shard_map/forward_product/pallas_call | solution.py:72
  125.0 9.4 %forward_product.8 = f32[2,1032,128]{2,1,0:T(8,128)S(1)} custom-call(s32[3]{0:T(128)S(1)} %pad_add_fusion.5.index_ref, f32[512,128]{1,0:T(8,128)S(1)} %slice_add_fusion.6.refs_0_, f32[512,128]{1,0:T(8,128)S(1)} %collective-permute-done.10.refs_1_, f32[512,128]{1,0:T(8,128)S(1)} %collective-permute-done.11.refs_2_, ...), custom_call_target="tpu_custom_call" | custom-call | flops 3221225472 | bytes 16777216 | tf_op jit(solution)/shard_map/forward_product/pallas_call | solution.py:72
  136.4 9.4 %forward_product.6 = f32[2,1032,128]{2,1,0:T(8,128)S(1)} custom-call(s32[3]{0:T(128)S(1)} %pad_add_fusion.index_ref, f32[512,128]{1,0:T(8,128)S(1)} %slice_add_fusion.6.refs_0_, f32[512,128]{1,0:T(8,128)S(1)} %collective-permute-done.10.refs_1_, f32[512,128]{1,0:T(8,128)S(1)} %collective-permute-done.11.refs_2_, ...), custom_call_target="tpu_custom_call" | custom-call | flops 3221225472 | bytes 16777216 | tf_op jit(solution)/shard_map/forward_product/pallas_call | solution.py:72
  151.3 7.7 %collective-permute-done.15 = f32[1,1032,128]{2,1,0:T(8,128)S(1)} collective-permute-done((f32[1,1032,128]{2,1,0:T(8,128)S(1)}, f32[1,1032,128]{2,1,0:T(8,128)S(1)}, u32[]{:S(2)}, u32[]{:S(2)}) %collective-permute-start.15) | collective-permute-done | bytes 528416 | tf_op jit(solution)/shard_map/ppermute | solution.py:232
  161.5 12.5 %collective-permute-done.16.refs_0_ = f32[1024,128]{1,0:T(8,128)S(1)} collective-permute-done((f32[1024,128]{1,0:T(8,128)S(1)}, f32[1024,128]{1,0:T(8,128)S(1)}, u32[]{:S(2)}, u32[]{:S(2)}) %collective-permute-start.16) | collective-permute-done | bytes 524320 | tf_op jit(solution)/shard_map/ppermute | solution.py:200
  174.5 9.4 %adjoint_product.12 = (f32[128,2048]{1,0:T(8,128)S(1)}, f32[8,128]{1,0:T(8,128)S(1)}) custom-call(s32[3]{0:T(128)S(1)} %pad_add_fusion.3.index_ref, f32[1024,128]{1,0:T(8,128)S(1)} %slice_bitcast_fusion.1.refs_0_, f32[1024,128]{1,0:T(8,128)S(1)} %collective-permute-done.22.refs_1_, f32[8192,2048]{1,0:T(8,128)} %refs_2_.11), custom_call_target="tpu_custom_call" | custom-call | flops 3221225472 | bytes 16777216 | tf_op jit(solution)/shard_map/adjoint_product/pallas_call | solution.py:156
  185.0 16.8 %adjoint_product.13 = (f32[128,2048]{1,0:T(8,128)S(1)}, f32[8,128]{1,0:T(8,128)S(1)}) custom-call(s32[5]{0:T(128)S(1)} %pad_add_fusion.2.index_ref, f32[1024,128]{1,0:T(8,128)S(1)} %collective-permute-done.16.refs_0_, f32[1024,128]{1,0:T(8,128)S(1)} %collective-permute-done.19.refs_1_, f32[1024,128]{1,0:T(8,128)S(1)} %collective-permute-done.20.refs_2_, ...), custom_call_target="tpu_custom_call" | custom-call | flops 6442450944 | bytes 33554432 | tf_op jit(solution)/shard_map/adjoint_product/pallas_call | solution.py:156
  201.8 9.7 %adjoint_product.14 = f32[4,520,128]{2,1,0:T(8,128)S(1)} custom-call(s32[3]{0:T(128)S(1)} %pad_add_fusion.1.index_ref, f32[1024,128]{1,0:T(8,128)S(1)} %collective-permute-done.17.refs_0_, f32[1024,128]{1,0:T(8,128)S(1)} %collective-permute-done.18.refs_1_, f32[8192,2048]{1,0:T(8,128)} %refs_2_.11, f32[128,2048]{1,0:T(8,128)S(1)} %get-tuple-element.21.refs_3_, ...), custom_call_target="tpu_custom_call" | custom-call | flops 3221225472 | bytes 16777216 | tf_op jit(solution)/shard_map/adjoint_product/pallas_call | solution.py:156
  218.1 9.8 %collective-permute-done.23 = f32[520,128]{1,0:T(8,128)S(1)} collective-permute-done((f32[520,128]{1,0:T(8,128)S(1)}, f32[520,128]{1,0:T(8,128)S(1)}, u32[]{:S(2)}, u32[]{:S(2)}) %collective-permute-start.23) | collective-permute-done | bytes 266272 | tf_op jit(solution)/shard_map/ppermute | solution.py:219
  228.0 9.3 %collective-permute-done.24 = f32[520,128]{1,0:T(8,128)S(1)} collective-permute-done((f32[520,128]{1,0:T(8,128)S(1)}, f32[520,128]{1,0:T(8,128)S(1)}, u32[]{:S(2)}, u32[]{:S(2)}) %collective-permute-start.24) | collective-permute-done | bytes 266272 | tf_op jit(solution)/shard_map/ppermute | solution.py:219
  237.4 5.6 %collective-permute-start.26 = (f32[512,128]{1,0:T(8,128)S(1)}, f32[512,128]{1,0:T(8,128)S(1)}, u32[]{:S(2)}, u32[]{:S(2)}) collective-permute-start(f32[512,128]{1,0:T(8,128)S(1)} %fusion.10.refs_0_), channel_id=1, source_target_pairs={{0,8},{8,0},{16,24},{24,16},{1,9},{9,1},{17,25},{25,17},{2,10},{10... | collective-permute-start | bytes 786440 | tf_op jit(solution)/shard_map/ppermute | solution.py:224
  245.5 8.0 %collective-permute-done.26.refs_1_ = f32[512,128]{1,0:T(8,128)S(1)} collective-permute-done((f32[512,128]{1,0:T(8,128)S(1)}, f32[512,128]{1,0:T(8,128)S(1)}, u32[]{:S(2)}, u32[]{:S(2)}) %collective-permute-start.26) | collective-permute-done | bytes 262176 | tf_op jit(solution)/shard_map/ppermute | solution.py:224
  253.4 10.9 %collective-permute-done.27.refs_2_ = f32[512,128]{1,0:T(8,128)S(1)} collective-permute-done((f32[512,128]{1,0:T(8,128)S(1)}, f32[512,128]{1,0:T(8,128)S(1)}, u32[]{:S(2)}, u32[]{:S(2)}) %collective-permute-start.27) | collective-permute-done | bytes 262176 | tf_op jit(solution)/shard_map/ppermute | solution.py:224
  264.4 16.7 %forward_product.10 = f32[4,1032,128]{2,1,0:T(8,128)S(1)} custom-call(s32[5]{0:T(128)S(1)} %pad_add_fusion.4.index_ref, f32[512,128]{1,0:T(8,128)S(1)} %fusion.10.refs_0_, f32[512,128]{1,0:T(8,128)S(1)} %collective-permute-done.26.refs_1_, f32[512,128]{1,0:T(8,128)S(1)} %collective-permute-done.27.refs_2_, f32[512,128]{1,0:T(8,128)S(1)} %collective-permute-done.28.refs_3_, ...), custom_call_target="tpu_custom_call" | custom-call | flops 6442450944 | bytes 33554432 | tf_op jit(solution)/shard_map/forward_product/pallas_call | solution.py:72
  281.1 9.4 %forward_product.11 = f32[2,1032,128]{2,1,0:T(8,128)S(1)} custom-call(s32[3]{0:T(128)S(1)} %pad_add_fusion.5.index_ref, f32[512,128]{1,0:T(8,128)S(1)} %fusion.10.refs_0_, f32[512,128]{1,0:T(8,128)S(1)} %collective-permute-done.26.refs_1_, f32[512,128]{1,0:T(8,128)S(1)} %collective-permute-done.27.refs_2_, f32[512,128]{1,0:T(8,128)S(1)} %collective-permute-done.28.refs_3_, ...), custom_call_target="tpu_custom_call" | custom-call | flops 3221225472 | bytes 16777216 | tf_op jit(solution)/shard_map/forward_product/pallas_call | solution.py:72
  292.7 9.4 %forward_product.9 = f32[2,1032,128]{2,1,0:T(8,128)S(1)} custom-call(s32[3]{0:T(128)S(1)} %pad_add_fusion.index_ref, f32[512,128]{1,0:T(8,128)S(1)} %fusion.10.refs_0_, f32[512,128]{1,0:T(8,128)S(1)} %collective-permute-done.26.refs_1_, f32[512,128]{1,0:T(8,128)S(1)} %collective-permute-done.27.refs_2_, f32[512,128]{1,0:T(8,128)S(1)} %collective-permute-done.28.refs_3_, ...), custom_call_target="tpu_custom_call" | custom-call | flops 3221225472 | bytes 16777216 | tf_op jit(solution)/shard_map/forward_product/pallas_call | solution.py:72
  307.5 7.6 %collective-permute-done.31 = f32[1,1032,128]{2,1,0:T(8,128)S(1)} collective-permute-done((f32[1,1032,128]{2,1,0:T(8,128)S(1)}, f32[1,1032,128]{2,1,0:T(8,128)S(1)}, u32[]{:S(2)}, u32[]{:S(2)}) %collective-permute-start.31) | collective-permute-done | bytes 528416 | tf_op jit(solution)/shard_map/ppermute | solution.py:232
  318.6 11.5 %collective-permute-done.32.refs_0_ = f32[1024,128]{1,0:T(8,128)S(1)} collective-permute-done((f32[1024,128]{1,0:T(8,128)S(1)}, f32[1024,128]{1,0:T(8,128)S(1)}, u32[]{:S(2)}, u32[]{:S(2)}) %collective-permute-start.32) | collective-permute-done | bytes 524320 | tf_op jit(solution)/shard_map/ppermute | solution.py:200
  331.3 9.4 %adjoint_product.15 = (f32[128,2048]{1,0:T(8,128)S(1)}, f32[8,128]{1,0:T(8,128)S(1)}) custom-call(s32[3]{0:T(128)S(1)} %pad_add_fusion.3.index_ref, f32[1024,128]{1,0:T(8,128)S(1)} %fusion.2.refs_0_, f32[1024,128]{1,0:T(8,128)S(1)} %collective-permute-done.38.refs_1_, f32[8192,2048]{1,0:T(8,128)} %refs_2_.11), custom_call_target="tpu_custom_call" | custom-call | flops 3221225472 | bytes 16777216 | tf_op jit(solution)/shard_map/adjoint_product/pallas_call | solution.py:156
  341.8 16.8 %adjoint_product.16 = (f32[128,2048]{1,0:T(8,128)S(1)}, f32[8,128]{1,0:T(8,128)S(1)}) custom-call(s32[5]{0:T(128)S(1)} %pad_add_fusion.2.index_ref, f32[1024,128]{1,0:T(8,128)S(1)} %collective-permute-done.32.refs_0_, f32[1024,128]{1,0:T(8,128)S(1)} %collective-permute-done.35.refs_1_, f32[1024,128]{1,0:T(8,128)S(1)} %collective-permute-done.36.refs_2_, ...), custom_call_target="tpu_custom_call" | custom-call | flops 6442450944 | bytes 33554432 | tf_op jit(solution)/shard_map/adjoint_product/pallas_call | solution.py:156
  358.6 9.7 %adjoint_product.17 = f32[4,520,128]{2,1,0:T(8,128)S(1)} custom-call(s32[3]{0:T(128)S(1)} %pad_add_fusion.1.index_ref, f32[1024,128]{1,0:T(8,128)S(1)} %collective-permute-done.33.refs_0_, f32[1024,128]{1,0:T(8,128)S(1)} %collective-permute-done.34.refs_1_, f32[8192,2048]{1,0:T(8,128)} %refs_2_.11, f32[128,2048]{1,0:T(8,128)S(1)} %get-tuple-element.25.refs_3_, ...), custom_call_target="tpu_custom_call" | custom-call | flops 3221225472 | bytes 16777216 | tf_op jit(solution)/shard_map/adjoint_product/pallas_call | solution.py:156
  375.2 9.9 %collective-permute-done.39 = f32[520,128]{1,0:T(8,128)S(1)} collective-permute-done((f32[520,128]{1,0:T(8,128)S(1)}, f32[520,128]{1,0:T(8,128)S(1)}, u32[]{:S(2)}, u32[]{:S(2)}) %collective-permute-start.39) | collective-permute-done | bytes 266272 | tf_op jit(solution)/shard_map/ppermute | solution.py:219
  385.1 9.2 %collective-permute-done.40 = f32[520,128]{1,0:T(8,128)S(1)} collective-permute-done((f32[520,128]{1,0:T(8,128)S(1)}, f32[520,128]{1,0:T(8,128)S(1)}, u32[]{:S(2)}, u32[]{:S(2)}) %collective-permute-start.40) | collective-permute-done | bytes 266272 | tf_op jit(solution)/shard_map/ppermute | solution.py:219
  (109 shorter events, 64.3 us)
Async XLA Ops:
  0.6 19.2 %collective-permute-start.6 = (f32[1024,128]{1,0:T(8,128)}, f32[1024,128]{1,0:T(8,128)S(1)}, u32[]{:S(2)}, u32[]{:S(2)}) collective-permute-start(f32[1024,128]{1,0:T(8,128)} %refs_0_.1), channel_id=1, source_target_pairs={{0,1},{1,0},{2,3},{3,2},{4,5},{5,4},{6,7},{7,6},{8,9},{9,8},{10,11... | collective-permute-start | bytes 1572872 | tf_op jit(solution)/shard_map/ppermute | solution.py:201
  1.1 14.6 %collective-permute-start = (f32[1024,128]{1,0:T(8,128)}, f32[1024,128]{1,0:T(8,128)S(1)}, u32[]{:S(2)}, u32[]{:S(2)}) collective-permute-start(f32[1024,128]{1,0:T(8,128)} %refs_0_.1), channel_id=1, source_target_pairs={{0,4},{1,3},{2,6},{3,1},{4,0},{5,7},{6,2},{7,5},{8,12},{9,11},{10,... | collective-permute-start | bytes 1572872 | tf_op jit(solution)/shard_map/ppermute | solution.py:200
  3.7 14.5 %collective-permute-start.3 = (f32[1024,128]{1,0:T(8,128)}, f32[1024,128]{1,0:T(8,128)S(1)}, u32[]{:S(2)}, u32[]{:S(2)}) collective-permute-start(f32[1024,128]{1,0:T(8,128)} %refs_0_.1), channel_id=1, source_target_pairs={{0,2},{1,5},{2,0},{3,7},{4,6},{5,1},{6,4},{7,3},{8,10},{9,13},{10,... | collective-permute-start | bytes 1572872 | tf_op jit(solution)/shard_map/ppermute | solution.py:200
  15.8 15.7 %collective-permute-start.4 = (f32[1024,128]{1,0:T(8,128)S(1)}, f32[1024,128]{1,0:T(8,128)S(1)}, u32[]{:S(2)}, u32[]{:S(2)}) collective-permute-start(f32[1024,128]{1,0:T(8,128)S(1)} %collective-permute-done.refs_0_), channel_id=1, source_target_pairs={{0,1},{1,0},{2,3},{3,2},{4,5},{5,4},{6,7},{7,6},{8,9},{9,8},{10,11... | collective-permute-start | bytes 1572872 | tf_op jit(solution)/shard_map/ppermute | solution.py:201
  15.8 15.3 %collective-permute-start.1 = (f32[1024,128]{1,0:T(8,128)S(1)}, f32[1024,128]{1,0:T(8,128)S(1)}, u32[]{:S(2)}, u32[]{:S(2)}) collective-permute-start(f32[1024,128]{1,0:T(8,128)S(1)} %collective-permute-done.refs_0_), channel_id=1, source_target_pairs={{0,2},{1,5},{2,0},{3,7},{4,6},{5,1},{6,4},{7,3},{8,10},{9,13},{10,... | collective-permute-start | bytes 1572872 | tf_op jit(solution)/shard_map/ppermute | solution.py:200
  18.3 13.2 %collective-permute-start.5 = (f32[1024,128]{1,0:T(8,128)S(1)}, f32[1024,128]{1,0:T(8,128)S(1)}, u32[]{:S(2)}, u32[]{:S(2)}) collective-permute-start(f32[1024,128]{1,0:T(8,128)S(1)} %collective-permute-done.3.refs_1_), channel_id=1, source_target_pairs={{0,1},{1,0},{2,3},{3,2},{4,5},{5,4},{6,7},{7,6},{8,9},{9,8},{10,11... | collective-permute-start | bytes 1572872 | tf_op jit(solution)/shard_map/ppermute | solution.py:201
  31.1 17.2 %collective-permute-start.2 = (f32[1024,128]{1,0:T(8,128)S(1)}, f32[1024,128]{1,0:T(8,128)S(1)}, u32[]{:S(2)}, u32[]{:S(2)}) collective-permute-start(f32[1024,128]{1,0:T(8,128)S(1)} %collective-permute-done.1.refs_0_), channel_id=1, source_target_pairs={{0,1},{1,0},{2,3},{3,2},{4,5},{5,4},{6,7},{7,6},{8,9},{9,8},{10,11... | collective-permute-start | bytes 1572872 | tf_op jit(solution)/shard_map/ppermute | solution.py:201
  58.1 13.5 %collective-permute-start.7 = (f32[520,128]{1,0:T(8,128)S(1)}, f32[520,128]{1,0:T(8,128)S(1)}, u32[]{:S(2)}, u32[]{:S(2)}) collective-permute-start(f32[520,128]{1,0:T(8,128)S(1)} %get-tuple-element.36), channel_id=1, source_target_pairs={{0,8},{8,0},{16,24},{24,16},{1,9},{9,1},{17,25},{25,17},{2,10},{10... | collective-permute-start | bytes 798728 | tf_op jit(solution)/shard_map/ppermute | solution.py:219
  59.9 21.6 %collective-permute-start.8 = (f32[520,128]{1,0:T(8,128)S(1)}, f32[520,128]{1,0:T(8,128)S(1)}, u32[]{:S(2)}, u32[]{:S(2)}) collective-permute-start(f32[520,128]{1,0:T(8,128)S(1)} %get-tuple-element.35), channel_id=1, source_target_pairs={{0,16},{8,24},{16,0},{24,8},{1,17},{9,25},{17,1},{25,9},{2,18},{10... | collective-permute-start | bytes 798728 | tf_op jit(solution)/shard_map/ppermute | solution.py:219
  62.5 19.0 %collective-permute-start.9 = (f32[520,128]{1,0:T(8,128)S(1)}, f32[520,128]{1,0:T(8,128)S(1)}, u32[]{:S(2)}, u32[]{:S(2)}) collective-permute-start(f32[520,128]{1,0:T(8,128)S(1)} %get-tuple-element.34), channel_id=1, source_target_pairs={{0,24},{8,16},{16,8},{24,0},{1,25},{9,17},{17,9},{25,1},{2,26},{10... | collective-permute-start | bytes 798728 | tf_op jit(solution)/shard_map/ppermute | solution.py:219
  81.7 14.8 %collective-permute-start.10 = (f32[512,128]{1,0:T(8,128)S(1)}, f32[512,128]{1,0:T(8,128)S(1)}, u32[]{:S(2)}, u32[]{:S(2)}) collective-permute-start(f32[512,128]{1,0:T(8,128)S(1)} %slice_add_fusion.6.refs_0_), channel_id=1, source_target_pairs={{0,8},{8,0},{16,24},{24,16},{1,9},{9,1},{17,25},{25,17},{2,10},{10... | collective-permute-start | bytes 786440 | tf_op jit(solution)/shard_map/ppermute | solution.py:224
  86.8 21.4 %collective-permute-start.11 = (f32[512,128]{1,0:T(8,128)S(1)}, f32[512,128]{1,0:T(8,128)S(1)}, u32[]{:S(2)}, u32[]{:S(2)}) collective-permute-start(f32[512,128]{1,0:T(8,128)S(1)} %slice_add_fusion.6.refs_0_), channel_id=1, source_target_pairs={{0,16},{8,24},{16,0},{24,8},{1,17},{9,25},{17,1},{25,9},{2,18},{10... | collective-permute-start | bytes 786440 | tf_op jit(solution)/shard_map/ppermute | solution.py:224
  87.9 20.3 %collective-permute-start.12 = (f32[512,128]{1,0:T(8,128)S(1)}, f32[512,128]{1,0:T(8,128)S(1)}, u32[]{:S(2)}, u32[]{:S(2)}) collective-permute-start(f32[512,128]{1,0:T(8,128)S(1)} %slice_add_fusion.6.refs_0_), channel_id=1, source_target_pairs={{0,24},{8,16},{16,8},{24,0},{1,25},{9,17},{17,9},{25,1},{2,26},{10... | collective-permute-start | bytes 786440 | tf_op jit(solution)/shard_map/ppermute | solution.py:224
  134.5 15.0 %collective-permute-start.14 = (f32[2,1032,128]{2,1,0:T(8,128)S(1)}, f32[2,1032,128]{2,1,0:T(8,128)S(1)}, u32[]{:S(2)}, u32[]{:S(2)}) collective-permute-start(f32[2,1032,128]{2,1,0:T(8,128)S(1)} %slice_add_fusion.2), channel_id=1, source_target_pairs={{0,2},{1,5},{2,0},{3,7},{4,6},{5,1},{6,4},{7,3},{8,10},{9,13},{10,... | collective-permute-start | bytes 3170312 | tf_op jit(solution)/shard_map/ppermute | solution.py:232
  159.2 14.8 %collective-permute-start.16 = (f32[1024,128]{1,0:T(8,128)S(1)}, f32[1024,128]{1,0:T(8,128)S(1)}, u32[]{:S(2)}, u32[]{:S(2)}) collective-permute-start(f32[1024,128]{1,0:T(8,128)S(1)} %slice_bitcast_fusion.1.refs_0_), channel_id=1, source_target_pairs={{0,4},{1,3},{2,6},{3,1},{4,0},{5,7},{6,2},{7,5},{8,12},{9,11},{10,... | collective-permute-start | bytes 1572872 | tf_op jit(solution)/shard_map/ppermute | solution.py:200
  160.8 13.2 %collective-permute-start.19 = (f32[1024,128]{1,0:T(8,128)S(1)}, f32[1024,128]{1,0:T(8,128)S(1)}, u32[]{:S(2)}, u32[]{:S(2)}) collective-permute-start(f32[1024,128]{1,0:T(8,128)S(1)} %slice_bitcast_fusion.1.refs_0_), channel_id=1, source_target_pairs={{0,2},{1,5},{2,0},{3,7},{4,6},{5,1},{6,4},{7,3},{8,10},{9,13},{10,... | collective-permute-start | bytes 1572872 | tf_op jit(solution)/shard_map/ppermute | solution.py:200
  161.5 13.0 %collective-permute-start.22 = (f32[1024,128]{1,0:T(8,128)S(1)}, f32[1024,128]{1,0:T(8,128)S(1)}, u32[]{:S(2)}, u32[]{:S(2)}) collective-permute-start(f32[1024,128]{1,0:T(8,128)S(1)} %slice_bitcast_fusion.1.refs_0_), channel_id=1, source_target_pairs={{0,1},{1,0},{2,3},{3,2},{4,5},{5,4},{6,7},{7,6},{8,9},{9,8},{10,11... | collective-permute-start | bytes 1572872 | tf_op jit(solution)/shard_map/ppermute | solution.py:201
  184.9 16.9 %collective-permute-start.18 = (f32[1024,128]{1,0:T(8,128)S(1)}, f32[1024,128]{1,0:T(8,128)S(1)}, u32[]{:S(2)}, u32[]{:S(2)}) collective-permute-start(f32[1024,128]{1,0:T(8,128)S(1)} %collective-permute-done.17.refs_0_), channel_id=1, source_target_pairs={{0,1},{1,0},{2,3},{3,2},{4,5},{5,4},{6,7},{7,6},{8,9},{9,8},{10,11... | collective-permute-start | bytes 1572872 | tf_op jit(solution)/shard_map/ppermute | solution.py:201
  211.6 16.4 %collective-permute-start.23 = (f32[520,128]{1,0:T(8,128)S(1)}, f32[520,128]{1,0:T(8,128)S(1)}, u32[]{:S(2)}, u32[]{:S(2)}) collective-permute-start(f32[520,128]{1,0:T(8,128)S(1)} %get-tuple-element.30), channel_id=1, source_target_pairs={{0,8},{8,0},{16,24},{24,16},{1,9},{9,1},{17,25},{25,17},{2,10},{10... | collective-permute-start | bytes 798728 | tf_op jit(solution)/shard_map/ppermute | solution.py:219
  215.6 21.6 %collective-permute-start.24 = (f32[520,128]{1,0:T(8,128)S(1)}, f32[520,128]{1,0:T(8,128)S(1)}, u32[]{:S(2)}, u32[]{:S(2)}) collective-permute-start(f32[520,128]{1,0:T(8,128)S(1)} %get-tuple-element.32), channel_id=1, source_target_pairs={{0,16},{8,24},{16,0},{24,8},{1,17},{9,25},{17,1},{25,9},{2,18},{10... | collective-permute-start | bytes 798728 | tf_op jit(solution)/shard_map/ppermute | solution.py:219
  216.7 20.5 %collective-permute-start.25 = (f32[520,128]{1,0:T(8,128)S(1)}, f32[520,128]{1,0:T(8,128)S(1)}, u32[]{:S(2)}, u32[]{:S(2)}) collective-permute-start(f32[520,128]{1,0:T(8,128)S(1)} %get-tuple-element.31), channel_id=1, source_target_pairs={{0,24},{8,16},{16,8},{24,0},{1,25},{9,17},{17,9},{25,1},{2,26},{10... | collective-permute-start | bytes 798728 | tf_op jit(solution)/shard_map/ppermute | solution.py:219
  237.4 16.0 %collective-permute-start.26 = (f32[512,128]{1,0:T(8,128)S(1)}, f32[512,128]{1,0:T(8,128)S(1)}, u32[]{:S(2)}, u32[]{:S(2)}) collective-permute-start(f32[512,128]{1,0:T(8,128)S(1)} %fusion.10.refs_0_), channel_id=1, source_target_pairs={{0,8},{8,0},{16,24},{24,16},{1,9},{9,1},{17,25},{25,17},{2,10},{10... | collective-permute-start | bytes 786440 | tf_op jit(solution)/shard_map/ppermute | solution.py:224
  243.0 21.4 %collective-permute-start.27 = (f32[512,128]{1,0:T(8,128)S(1)}, f32[512,128]{1,0:T(8,128)S(1)}, u32[]{:S(2)}, u32[]{:S(2)}) collective-permute-start(f32[512,128]{1,0:T(8,128)S(1)} %fusion.10.refs_0_), channel_id=1, source_target_pairs={{0,16},{8,24},{16,0},{24,8},{1,17},{9,25},{17,1},{25,9},{2,18},{10... | collective-permute-start | bytes 786440 | tf_op jit(solution)/shard_map/ppermute | solution.py:224
  244.1 20.3 %collective-permute-start.28 = (f32[512,128]{1,0:T(8,128)S(1)}, f32[512,128]{1,0:T(8,128)S(1)}, u32[]{:S(2)}, u32[]{:S(2)}) collective-permute-start(f32[512,128]{1,0:T(8,128)S(1)} %fusion.10.refs_0_), channel_id=1, source_target_pairs={{0,24},{8,16},{16,8},{24,0},{1,25},{9,17},{17,9},{25,1},{2,26},{10... | collective-permute-start | bytes 786440 | tf_op jit(solution)/shard_map/ppermute | solution.py:224
  290.7 14.9 %collective-permute-start.30 = (f32[2,1032,128]{2,1,0:T(8,128)S(1)}, f32[2,1032,128]{2,1,0:T(8,128)S(1)}, u32[]{:S(2)}, u32[]{:S(2)}) collective-permute-start(f32[2,1032,128]{2,1,0:T(8,128)S(1)} %slice_add_fusion), channel_id=1, source_target_pairs={{0,2},{1,5},{2,0},{3,7},{4,6},{5,1},{6,4},{7,3},{8,10},{9,13},{10,... | collective-permute-start | bytes 3170312 | tf_op jit(solution)/shard_map/ppermute | solution.py:232
  315.3 14.8 %collective-permute-start.32 = (f32[1024,128]{1,0:T(8,128)S(1)}, f32[1024,128]{1,0:T(8,128)S(1)}, u32[]{:S(2)}, u32[]{:S(2)}) collective-permute-start(f32[1024,128]{1,0:T(8,128)S(1)} %fusion.2.refs_0_), channel_id=1, source_target_pairs={{0,4},{1,3},{2,6},{3,1},{4,0},{5,7},{6,2},{7,5},{8,12},{9,11},{10,... | collective-permute-start | bytes 1572872 | tf_op jit(solution)/shard_map/ppermute | solution.py:200
  317.0 13.8 %collective-permute-start.35 = (f32[1024,128]{1,0:T(8,128)S(1)}, f32[1024,128]{1,0:T(8,128)S(1)}, u32[]{:S(2)}, u32[]{:S(2)}) collective-permute-start(f32[1024,128]{1,0:T(8,128)S(1)} %fusion.2.refs_0_), channel_id=1, source_target_pairs={{0,2},{1,5},{2,0},{3,7},{4,6},{5,1},{6,4},{7,3},{8,10},{9,13},{10,... | collective-permute-start | bytes 1572872 | tf_op jit(solution)/shard_map/ppermute | solution.py:200
  318.6 12.7 %collective-permute-start.38 = (f32[1024,128]{1,0:T(8,128)S(1)}, f32[1024,128]{1,0:T(8,128)S(1)}, u32[]{:S(2)}, u32[]{:S(2)}) collective-permute-start(f32[1024,128]{1,0:T(8,128)S(1)} %fusion.2.refs_0_), channel_id=1, source_target_pairs={{0,1},{1,0},{2,3},{3,2},{4,5},{5,4},{6,7},{7,6},{8,9},{9,8},{10,11... | collective-permute-start | bytes 1572872 | tf_op jit(solution)/shard_map/ppermute | solution.py:201
  341.7 16.8 %collective-permute-start.34 = (f32[1024,128]{1,0:T(8,128)S(1)}, f32[1024,128]{1,0:T(8,128)S(1)}, u32[]{:S(2)}, u32[]{:S(2)}) collective-permute-start(f32[1024,128]{1,0:T(8,128)S(1)} %collective-permute-done.33.refs_0_), channel_id=1, source_target_pairs={{0,1},{1,0},{2,3},{3,2},{4,5},{5,4},{6,7},{7,6},{8,9},{9,8},{10,11... | collective-permute-start | bytes 1572872 | tf_op jit(solution)/shard_map/ppermute | solution.py:201
  368.4 16.7 %collective-permute-start.39 = (f32[520,128]{1,0:T(8,128)S(1)}, f32[520,128]{1,0:T(8,128)S(1)}, u32[]{:S(2)}, u32[]{:S(2)}) collective-permute-start(f32[520,128]{1,0:T(8,128)S(1)} %get-tuple-element.27), channel_id=1, source_target_pairs={{0,8},{8,0},{16,24},{24,16},{1,9},{9,1},{17,25},{25,17},{2,10},{10... | collective-permute-start | bytes 798728 | tf_op jit(solution)/shard_map/ppermute | solution.py:219
  372.7 21.6 %collective-permute-start.40 = (f32[520,128]{1,0:T(8,128)S(1)}, f32[520,128]{1,0:T(8,128)S(1)}, u32[]{:S(2)}, u32[]{:S(2)}) collective-permute-start(f32[520,128]{1,0:T(8,128)S(1)} %get-tuple-element.29), channel_id=1, source_target_pairs={{0,16},{8,24},{16,0},{24,8},{1,17},{9,25},{17,1},{25,9},{2,18},{10... | collective-permute-start | bytes 798728 | tf_op jit(solution)/shard_map/ppermute | solution.py:219
  373.8 20.5 %collective-permute-start.41 = (f32[520,128]{1,0:T(8,128)S(1)}, f32[520,128]{1,0:T(8,128)S(1)}, u32[]{:S(2)}, u32[]{:S(2)}) collective-permute-start(f32[520,128]{1,0:T(8,128)S(1)} %get-tuple-element.28), channel_id=1, source_target_pairs={{0,24},{8,16},{16,8},{24,0},{1,25},{9,17},{17,9},{25,1},{2,26},{10... | collective-permute-start | bytes 798728 | tf_op jit(solution)/shard_map/ppermute | solution.py:219
  (15 other events, 134.2 us)
